TPU v7x, 32 devices: a whole 2x2x4 slice. The times are simulated.
32 devices in a mesh: unit: 8 (over z, x), day: 4 (over y, core).
Axes of the slice: x: 2, y: 2, z: 4, core: 2. Of those that a mesh axis runs over, the one named last changes fastest.
Arguments:
- outcomes: float32 [32768, 1024], P('unit', 'day'), may hold values from -6 to 6
- cohort: int32 [32768], P('unit'), may hold values from 0 to 8
- pre_end: int32 [8], replicated, may hold values from 256 to 511
- post_start: int32 [8], replicated, may hold values from 512 to 767
- unit_logit: float32 [8, 32768], P(None, 'unit'), may hold values from -4 to 4
- time_logit: float32 [8, 1024], P(None, 'day'), may hold values from -4 to 4
Outputs:
- unit_weights: float32 [8, 32768], P(None, 'unit')
- time_weights: float32 [8, 1024], P(None, 'day')
All inputs are finite; a program needn't handle non-finite values.
Results may differ from a plain program's by a relative error of at most 0.0003.
Values sent between devices are 32-bit elements; how exact they have to be, the bound alone decides.
No kernel may reach another device: no remote copies, remote signals or barrier semaphores. Data moves between devices by JAX's collectives and lax.ppermute only.
A program may use at most 64 MiB of HBM per device.

v0:
```python
import jax
import jax.numpy as jnp
from jax import lax
from jax.sharding import PartitionSpec as P

highest = lax.Precision.HIGHEST
step_rate = 16.0


def weigh_rows(left, outcomes):
    return jnp.dot(left, outcomes, precision=highest, preferred_element_type=jnp.float32)


def weigh_days(left, outcomes):
    return lax.dot_general(
        left,
        outcomes,
        (((1,), (1,)), ((), ())),
        precision=highest,
        preferred_element_type=jnp.float32,
    )


def local(outcomes, cohort, pre_end, post_start, unit_logit, time_logit):
    groups = pre_end.shape[0]
    unit_rows, day_cols = outcomes.shape
    day_devices = lax.axis_size("day")
    all_count = day_devices * day_cols
    labels = jnp.arange(groups, dtype=jnp.int32)[:, None]
    treated = (cohort[None, :] == labels).astype(jnp.float32)
    control = (cohort[None, :] > labels).astype(jnp.float32)
    day_start = lax.axis_index("day") * day_cols
    day_index = day_start + jnp.arange(day_cols, dtype=jnp.int32)[None, :]
    before = (day_index < pre_end[:, None]).astype(jnp.float32)
    before_len = pre_end.astype(jnp.float32)
    after_len = (all_count - post_start).astype(jnp.float32)
    raised = jnp.exp(unit_logit) * control
    unit_norm, treat_count, ctrl_count, fitted, treat_sum = lax.psum(
        (
            jnp.sum(raised, axis=1),
            jnp.sum(treated, axis=1),
            jnp.sum(control, axis=1),
            weigh_rows(raised, outcomes),
            weigh_rows(treated, outcomes),
        ),
        "unit",
    )
    weights = raised / unit_norm[:, None]
    fitted = fitted / unit_norm[:, None]
    residual = (fitted - treat_sum / jnp.maximum(treat_count, 1.0)[:, None]) * before
    ctrl_root = jnp.sqrt(jnp.maximum(ctrl_count, 1.0))[:, None]
    relaid = lax.all_to_all(outcomes, "day", split_axis=0, concat_axis=1, tiled=True)
    slab_rows = unit_rows // day_devices
    full_resid, full_logit = (
        lax.all_gather(residual, "day", axis=1, tiled=True),
        lax.all_gather(time_logit, "day", axis=1, tiled=True),
    )
    all_days = jnp.arange(all_count, dtype=jnp.int32)[None, :]
    full_before = (all_days < pre_end[:, None]).astype(jnp.float32)
    full_after = (all_days >= post_start[:, None]).astype(jnp.float32)
    row_start = lax.axis_index("day") * slab_rows
    sub_control = lax.dynamic_slice_in_dim(control, row_start, slab_rows, 1)
    sub_weights = lax.dynamic_slice_in_dim(weights, row_start, slab_rows, 1)
    unit_grad = weigh_days(full_resid, relaid)
    updated = sub_weights * jnp.exp(-step_rate * unit_grad / jnp.sqrt(before_len)[:, None])
    unit_total = lax.psum(jnp.sum(updated, axis=1), ("unit", "day"))
    row_share = updated / unit_total[:, None] * ctrl_count[:, None]
    unit_weights = lax.all_gather(row_share, "day", axis=1, tiled=True)
    time_raised = jnp.exp(full_logit) * full_before
    time_lam = time_raised / jnp.sum(time_raised, axis=1)[:, None]
    time_fit = weigh_days(time_lam, relaid)
    post_sum = weigh_days(full_after, relaid)
    shortfall = (time_fit - post_sum / after_len[:, None]) * sub_control
    time_grad = lax.psum(weigh_rows(shortfall, relaid), ("unit", "day"))
    moved = time_lam * jnp.exp(-step_rate * time_grad / ctrl_root)
    full_weights = moved / jnp.sum(moved, axis=1)[:, None] * before_len[:, None]
    time_weights = lax.dynamic_slice_in_dim(full_weights, day_start, day_cols, 1)
    return (unit_weights, time_weights)


def solution(mesh):
    return jax.shard_map(
        local,
        mesh=mesh,
        in_specs=(P("unit", "day"), P("unit"), P(), P(), P(None, "unit"), P(None, "day")),
        out_specs=(P(None, "unit"), P(None, "day")),
        check_vma=False,
    )
```

profile of v0, /device:TPU:0, one launch (start us, length us, event | category | flops | bytes accessed | tf_op | source)
XLA Modules:
  0.0 126.4 jit_solution(16319792062546472342)
XLA Ops:
  0.6 0.0 copy-start.4
  0.6 0.0 copy-start.2
  0.7 0.0 copy-start.3
  0.7 5.0 %all-to-all-start = ((f32[4,1024,256]{2,1,0:T(8,128)}), f32[4,1024,256]{2,1,0:T(8,128)}, u32[]{:S(2)}, u32[]{:S(2)}) async-start(f32[4,1024,256]{2,1,0:T(8,128)} %bitcast.16), calls=%async_computation | async-start | bytes 8388608 | tf_op jit(solution)/shard_map/all_to_all | solution.py:52
  5.7 0.0 copy-done.4
  5.7 0.0 copy-done.2
  5.7 0.0 copy-done.3
  5.7 0.0 copy-start.1
  5.7 0.2 fusion.8
  5.9 0.0 copy-start.5
  5.9 0.0 copy-start.6
  5.9 3.8 %fusion.5 = f32[8,256]{1,0:T(8,128)S(1)} fusion(f32[4096,256]{1,0:T(8,128)} %param.6, s32[4096]{0:T(1024)S(1)} %copy-done.2), kind=kOutput, calls=%fused_computation.9 | convolution fusion | flops 100696064 | bytes 4218880 | tf_op jit(solution)/shard_map/dot_general | solution.py:11
  9.7 0.0 copy-done.1
  9.7 1.7 %fusion.18 = f32[8,256]{1,0:T(8,128)S(1)} fusion(f32[8,4096]{1,0:T(8,128)S(1)} %get-tuple-element.16, f32[4096,256]{1,0:T(8,128)S(1)} %copy-done.1), kind=kOutput, calls=%fused_computation.36 | convolution fusion | flops 100663296 | bytes 4333568 | tf_op jit(solution)/shard_map/dot_general | solution.py:11
  11.5 38.8 %all-reduce.1 = (f32[8,256]{1,0:T(8,128)S(1)}, f32[8,256]{1,0:T(8,128)S(1)}, f32[8]{0:T(128)S(1)}, f32[8]{0:T(128)S(1)}, f32[8]{0:T(128)S(1)}) all-reduce(f32[8,256]{1,0:T(8,128)S(1)} %fusion.5, f32[8,256]{1,0:T(8,128)S(1)} %fusion.18, f32[8]{0:T(128)S(1)} %get-tuple-element.3, ...), channel_id=1, replica_groups=mesh['unit'=8,'day'=4] {'unit'}, use_global_device_ids=true, to_apply=%region_3.0 | all-reduce | flops 4120 | bytes 32960 | tf_op jit(solution)/shard_map/psum | solution.py:38
  50.3 0.0 copy-done.5
  50.3 5.2 %all_gather.11 = f32[8,1024]{1,0:T(8,128)S(1)} all-gather(f32[8,256]{1,0:T(8,128)S(1)} %copy-done.5), channel_id=1, replica_groups=mesh['unit'=8,'day'=4] {'day'}, dimensions={1}, use_global_device_ids=true | all-gather | bytes 40960 | tf_op jit(solution)/shard_map/all_gather | solution.py:56
  55.5 0.1 subtract_select_fusion
  55.6 5.6 %all_gather.9 = f32[8,1024]{1,0:T(8,128)S(1)} all-gather(f32[8,256]{1,0:T(8,128)S(1)} %subtract_select_fusion), channel_id=1, replica_groups=mesh['unit'=8,'day'=4] {'day'}, dimensions={1}, use_global_device_ids=true | all-gather | bytes 40960 | tf_op jit(solution)/shard_map/all_gather | solution.py:55
  61.1 0.2 fusion.10
  61.3 0.0 copy-done.6
  61.4 0.0 all-to-all-done
  61.4 5.4 %copy.8 = f32[1024,4,256]{0,2,1:T(8,128)} copy(f32[1024,4,256]{2,0,1:T(8,128)} %bitcast.1) | data formatting | bytes 8388608 | tf_op jit(solution)/shard_map/all_to_all | solution.py:52
  66.8 0.0 copy-start
  66.8 4.4 %fusion.13 = f32[8,1024]{1,0:T(8,128)S(1)} fusion(f32[1024,1024]{0,1:T(8,128)} %bitcast.12, f32[8,1024]{1,0:T(8,128)S(1)} %all_gather.11, f32[8]{0:T(128)S(1)} %fusion.10, s32[8]{0:T(128)S(1)} %copy-done.4), kind=kOutput, calls=%fused_computation.32 | convolution fusion | flops 100687872 | bytes 4259904 | tf_op jit(solution)/shard_map/dot_general | solution.py:15
  71.3 0.0 copy-done
  71.3 1.5 %fusion.1 = f32[8,1024]{1,0:T(8,128)S(1)} fusion(f32[8,1024]{1,0:T(8,128)S(1)} %fusion.13, f32[1024,1024]{0,1:T(8,128)S(1)} %bitcast.13, f32[8,4096]{1,0:T(8,128)S(1)} %fusion.6, s32[]{:T(128)S(6)} %select_n.7, f32[8]{0:T(128)S(1)} %subtract_convert_fusion, s32[8]{0:T(128)S(1)} %copy-done.6), kind=kOutput, calls=%fused_computation.2 | convolution fusion | flops 100696064 | bytes 4292676 | tf_op jit(solution)/shard_map/dot_general | solution.py:15
  72.8 3.6 %fusion.19 = f32[8,1024]{1,0:T(8,128)S(1)} fusion(f32[8,1024]{1,0:T(8,128)S(1)} %fusion.1, f32[1024,1024]{0,1:T(8,128)S(1)} %bitcast.14), kind=kOutput, calls=%fused_computation.37 | convolution fusion | flops 100663296 | bytes 4259840 | tf_op jit(solution)/shard_map/dot_general | solution.py:11
  76.4 2.2 %fusion.17 = (f32[8]{0:T(128)S(1)}, f32[8,1024]{1,0:T(8,128)S(1)}) fusion(f32[8]{0:T(128)S(1)} %convert_sqrt_fusion, f32[8,1024]{1,0:T(8,128)S(1)} %all_gather.9, f32[1024,1024]{0,1:T(8,128)S(1)} %bitcast.15, f32[8]{0:T(128)S(1)} %get-tuple-element.9, f32[8,4096]{1,0:T(8,128)S(1)} %get-tuple-element.16, s32[]{:T(128)S(6)} %select_n.7), kind=kOutput, calls=%fused_computation.35 | convolution fusion | flops 100704248 | bytes 4292708 | tf_op jit(solution)/shard_map/dot_general | solution.py:15
  78.6 40.5 %all-reduce = (f32[8]{0:T(128)S(1)}, f32[8,1024]{1,0:T(8,128)S(1)}) all-reduce(f32[8]{0:T(128)S(1)} %get-tuple-element.17, f32[8,1024]{1,0:T(8,128)S(1)} %fusion.19), channel_id=1, replica_groups=mesh['unit'=8,'day'=4] {'unit','day'}, use_global_device_ids=true, to_apply=%region_7.0 | all-reduce | flops 8200 | bytes 65600 | tf_op jit(solution)/shard_map/psum | solution.py:66
  119.1 0.2 fusion.15
  119.3 5.8 %all_gather.10 = f32[8,4096]{1,0:T(8,128)S(1)} all-gather(f32[8,1024]{1,0:T(8,128)S(1)} %get-tuple-element.19), channel_id=1, replica_groups=mesh['unit'=8,'day'=4] {'day'}, dimensions={1}, use_global_device_ids=true | all-gather | bytes 163840 | tf_op jit(solution)/shard_map/all_gather | solution.py:68
  125.1 0.7 fusion.12
  125.8 0.7 copy.10
  (7 shorter events, 0.0 us)
Async XLA Ops:
  0.6 5.0 %copy-start.4 = (s32[8]{0:T(128)S(1)}, s32[8]{0:T(128)}, u32[]{:S(2)}) copy-start(s32[8]{0:T(128)} %param.8) | copy-start | bytes 100
  0.6 5.1 %copy-start.2 = (s32[4096]{0:T(1024)S(1)}, s32[4096]{0:T(1024)}, u32[]{:S(2)}) copy-start(s32[4096]{0:T(1024)} %param.7) | copy-start | bytes 49156
  0.7 5.1 %copy-start.3 = (f32[8,4096]{1,0:T(8,128)S(1)}, f32[8,4096]{1,0:T(8,128)}, u32[]{:S(2)}) copy-start(f32[8,4096]{1,0:T(8,128)} %param.10) | copy-start | bytes 393220
  0.7 60.7 %all-to-all-start = ((f32[4,1024,256]{2,1,0:T(8,128)}), f32[4,1024,256]{2,1,0:T(8,128)}, u32[]{:S(2)}, u32[]{:S(2)}) async-start(f32[4,1024,256]{2,1,0:T(8,128)} %bitcast.16), calls=%async_computation | async-start | bytes 8388608 | tf_op jit(solution)/shard_map/all_to_all | solution.py:52
  5.7 4.0 %copy-start.1 = (f32[4096,256]{1,0:T(8,128)S(1)}, f32[4096,256]{1,0:T(8,128)}, u32[]{:S(2)}) copy-start(f32[4096,256]{1,0:T(8,128)} %param.6) | copy-start | bytes 12582916
  5.9 44.4 %copy-start.5 = (f32[8,256]{1,0:T(8,128)S(1)}, f32[8,256]{1,0:T(8,128)}, u32[]{:S(2)}) copy-start(f32[8,256]{1,0:T(8,128)} %param.11) | copy-start | bytes 24580
  5.9 55.4 %copy-start.6 = (s32[8]{0:T(128)S(1)}, s32[8]{0:T(128)}, u32[]{:S(2)}) copy-start(s32[8]{0:T(128)} %param.9) | copy-start | bytes 100
  66.8 4.4 %copy-start = (f32[1024,4,256]{0,2,1:T(8,128)S(1)}, f32[1024,4,256]{0,2,1:T(8,128)}, u32[]{:S(2)}) copy-start(f32[1024,4,256]{0,2,1:T(8,128)} %copy.8) | copy-start | bytes 12582916
where the time goes:
time: 127 us; the launch traced here: 126 us
  blocking collectives  95.9 us (76%)
  matrix products  17.3 us (14%)
  local copies, waits for them, and re-layouts  6.11 us (5%)
  starting transfers between devices  5 us (4%)
  other arithmetic  1.37 us (1%)
    psum x1, blocking collectives, local(): unit_total = lax.psum(jnp.sum(updated, axis=1), ('unit', 'day'))  40.5 us
    psum x1, blocking collectives, local(): lax.psum((jnp.sum(raised, axis=1), jnp.sum(treated, axis=1), jnp.sum(cont...  38.8 us
    dot_general x3, matrix products, weigh_rows(): jnp.dot(left, outcomes, precision=highest, preferred_element_type=jnp.flo...  9.09 us
    dot_general x3, matrix products, weigh_days(): lax.dot_general(left, outcomes, (((1,), (1,)), ((), ())), precision=highe...  8.18 us
    all_gather x1, blocking collectives, local(): unit_weights = lax.all_gather(row_share, 'day', axis=1, tiled=True)  5.8 us
    all_gather x1, blocking collectives, local(): lax.all_gather(residual, 'day', axis=1, tiled=True)  5.57 us
    all_to_all x1, local copies, waits for them, and re-layouts, local(): lax.all_to_all(outcomes, 'day', split_axis=0, concat_axis=1, tiled=True)  5.43 us
    all_gather x1, blocking collectives, local(): lax.all_gather(time_logit, 'day', axis=1, tiled=True)  5.19 us
  transfers between devices with their start and end apart: 1, of which 0 were waited for; matrix products, arithmetic and copies ran while one was open for 5% of the time, Pallas kernels for 0%

commit v1 on v0

v1 whole, which is shorter than its diff:
```python
import functools

import jax
import jax.numpy as jnp
from jax import lax
from jax.experimental import pallas as pl
from jax.experimental.pallas import tpu as pltpu
from jax.sharding import PartitionSpec as P

step_rate = 16.0
f32 = jnp.float32
bf16 = jnp.bfloat16
lanes = 128


def split_left(value):
    first = value.astype(bf16).astype(f32)
    rest = value - first
    second = rest.astype(bf16).astype(f32)
    return [first, second, rest - second]


def split_panel(value):
    high = value.astype(bf16)
    return high, (value - high.astype(f32)).astype(bf16)


def rows_dot(left, high, low):
    return jnp.dot(left, high, preferred_element_type=f32) + jnp.dot(left, low, preferred_element_type=f32)


def days_dot(left, high, low):
    dims = (((1,), (1,)), ((), ()))
    return lax.dot_general(left, high, dims, preferred_element_type=f32) + lax.dot_general(
        left, low, dims, preferred_element_type=f32
    )


def add_terms(stack, groups):
    return stack[:groups] + stack[groups : 2 * groups] + stack[2 * groups : 3 * groups]


def day_masks(day_axis, pre_end, post_start, groups, day_cols):
    start = lax.axis_index(day_axis) * day_cols
    days = start + lax.broadcasted_iota(jnp.int32, (groups, day_cols), 1)
    return days < pre_end, days >= post_start


def first_kernel(all_count, panel, cohort, pre_end, post_start, unit_logit, time_logit, sums, cross, raised_days):
    groups, day_cols = time_logit.shape
    before, after = day_masks("day", pre_end[...], post_start[...], groups, day_cols)
    raised_time = jnp.where(before, jnp.exp(time_logit[...]), 0.0)
    after_len = (all_count - post_start[...]).astype(f32)
    coef = raised_time - jnp.where(after, 1.0, 0.0) / after_len

    @pl.when(pl.program_id(0) == 0)
    def _():
        sums[...] = jnp.zeros_like(sums)
        raised_days[...] = raised_time

    rows = cohort.shape[1]
    label = lax.broadcasted_iota(jnp.int32, (groups, rows), 0)
    treated = jnp.where(cohort[...] == label, 1.0, 0.0)
    control = jnp.where(cohort[...] > label, 1.0, 0.0)
    raised = jnp.exp(unit_logit[...]) * control
    high, low = split_panel(panel[...])
    left = jnp.concatenate(split_left(raised) + [treated], axis=0).astype(bf16)
    product = rows_dot(left, high, low)
    sums[:groups, :] += add_terms(product, groups)
    sums[groups : 2 * groups, :] += product[3 * groups :]
    lane = lax.broadcasted_iota(jnp.int32, (groups, day_cols), 1)
    sums[2 * groups :, :] += jnp.where(
        lane == 0,
        jnp.sum(raised, axis=1, keepdims=True),
        jnp.where(
            lane == 1,
            jnp.sum(treated, axis=1, keepdims=True),
            jnp.where(lane == 2, jnp.sum(control, axis=1, keepdims=True), 0.0),
        ),
    )
    coef_terms = split_left(coef)
    left = jnp.concatenate(coef_terms + [jnp.zeros_like(coef)], axis=0).astype(bf16)
    cross[...] = add_terms(days_dot(left, high, low), groups)


def second_kernel(unit_devices, panel, sums, pre_end, post_start, cross, raised_days, pack, norms):
    groups, day_cols = raised_days.shape
    rows = panel.shape[0]
    unit_rows = cross.shape[1]
    step = pl.program_id(0)
    total = sums[pl.ds(0, 3 * groups), :]
    for other in range(1, unit_devices):
        total = total + sums[pl.ds(other * 3 * groups, 3 * groups), :]
    unit_norm = total[2 * groups :, 0:1]
    treat_count = jnp.maximum(total[2 * groups :, 1:2], 1.0)
    before, _ = day_masks("day", pre_end[...], post_start[...], groups, day_cols)
    gap = total[:groups] / unit_norm - total[groups : 2 * groups] / treat_count
    residual = jnp.where(before, gap, 0.0)

    @pl.when(step == 0)
    def _():
        norms[...] = total[2 * groups :, :lanes]
        pack[groups:, :unit_rows] = cross[...]
        pack[groups:, unit_rows:] = raised_days[...]
        pack[:groups, unit_rows:] = jnp.zeros_like(raised_days)

    high, low = split_panel(panel[...])
    left = jnp.concatenate(split_left(residual) + [jnp.zeros_like(residual)], axis=0).astype(bf16)
    here = pl.ds(pl.multiple_of(step * rows, rows), rows)
    pack[:groups, here] = add_terms(days_dot(left, high, low), groups)


def third_kernel(day_devices, panel, pack, norms, cohort, unit_logit, pre_end, updated, out):
    groups = unit_logit.shape[0]
    rows = panel.shape[0]
    day_cols = panel.shape[1]
    unit_rows = pack.shape[1] - day_cols
    step = pl.program_id(0)
    half = day_devices // 2
    here = pl.ds(pl.multiple_of(step * rows, rows), rows)

    def part(index, lower, where):
        return pack[pl.ds((2 * index + lower) * groups, groups), where]

    time_norm = jnp.zeros((groups, 1), f32)
    for index in range(half):
        time_norm += jnp.sum(part(index, 1, pl.ds(unit_rows, day_cols)), axis=1, keepdims=True)
    unit_grad = part(0, 0, here)
    time_fit = part(0, 1, here)
    post_mean = part(half, 1, here)
    for index in range(1, half):
        unit_grad = unit_grad + part(index, 0, here)
        time_fit = time_fit + part(index, 1, here)
        post_mean = post_mean + part(half + index, 1, here)
    label = lax.broadcasted_iota(jnp.int32, (groups, rows), 0)
    control = cohort[...] > label
    weights = jnp.where(control, jnp.exp(unit_logit[...]), 0.0) / norms[:, 0:1]
    root = jnp.sqrt(pre_end[...].astype(f32))
    new = weights * jnp.exp(unit_grad * (-step_rate / root))
    updated[...] = new
    shortfall = jnp.where(control, time_fit / time_norm + post_mean, 0.0)
    high, low = split_panel(panel[...])
    left = jnp.concatenate(split_left(shortfall) + [jnp.zeros_like(shortfall)], axis=0).astype(bf16)

    @pl.when(step == 0)
    def _():
        out[...] = jnp.zeros_like(out)

    out[:groups, :] += add_terms(rows_dot(left, high, low), groups)
    out[groups:, :] += jnp.broadcast_to(jnp.sum(new, axis=1, keepdims=True), (groups, day_cols))


def fourth_kernel(unit_devices, day_devices, gathered, updated, norms, pack, pre_end, unit_weights, time_weights):
    groups, unit_rows = updated.shape
    day_cols = time_weights.shape[1]
    own_day = lax.axis_index("day")
    half = day_devices // 2
    ctrl_count = norms[:, 2:3]
    root = jnp.sqrt(jnp.maximum(ctrl_count, 1.0))
    length = pre_end[...].astype(f32)

    def part(unit, day, lower):
        return gathered[pl.ds(((unit * day_devices + day) * 2 + lower) * groups, groups), :]

    unit_total = part(0, 0, 1)[:, 0:1]
    for unit in range(1, unit_devices):
        unit_total = unit_total + part(unit, 0, 1)[:, 0:1]
    unit_weights[...] = updated[...] * (ctrl_count / unit_total)
    time_norm = jnp.zeros((groups, 1), f32)
    raised = []
    for day in range(half):
        raised.append(pack[pl.ds((2 * day + 1) * groups, groups), pl.ds(unit_rows, day_cols)])
        time_norm += jnp.sum(raised[-1], axis=1, keepdims=True)
    moved_total = jnp.zeros((groups, 1), f32)
    own = jnp.zeros((groups, day_cols), f32)
    for day in range(half):
        grad = part(0, day, 0)
        for unit in range(1, unit_devices):
            grad = grad + part(unit, day, 0)
        moved = raised[day] / time_norm * jnp.exp(grad * (-step_rate / root))
        moved_total += jnp.sum(moved, axis=1, keepdims=True)
        own = jnp.where(own_day == day, moved, own)
    time_weights[...] = own * (length / moved_total)


def local(outcomes, cohort, pre_end, post_start, unit_logit, time_logit):
    groups = pre_end.shape[0]
    unit_rows, day_cols = outcomes.shape
    day_devices = lax.axis_size("day")
    unit_devices = lax.axis_size("unit")
    steps = 4
    rows = unit_rows // steps
    cohort = cohort[None, :]
    pre_end = pre_end[:, None]
    post_start = post_start[:, None]

    def whole(*shape):
        return pl.BlockSpec(shape, lambda i: (0,) * len(shape))

    panel_spec = pl.BlockSpec((rows, day_cols), lambda i: (i, 0))
    group_spec = pl.BlockSpec((groups, rows), lambda i: (0, i))
    label_spec = pl.BlockSpec((1, rows), lambda i: (0, i))
    end_spec = whole(groups, 1)
    days_spec = whole(groups, day_cols)
    params = pltpu.CompilerParams(vmem_limit_bytes=32 * 1024 * 1024)

    sums, cross, raised_days = pl.pallas_call(
        functools.partial(first_kernel, day_devices * day_cols),
        grid=(steps,),
        in_specs=[panel_spec, label_spec, end_spec, end_spec, group_spec, days_spec],
        out_specs=[whole(3 * groups, day_cols), group_spec, days_spec],
        out_shape=[
            jax.ShapeDtypeStruct((3 * groups, day_cols), f32),
            jax.ShapeDtypeStruct((groups, unit_rows), f32),
            jax.ShapeDtypeStruct((groups, day_cols), f32),
        ],
        compiler_params=params,
        name="first_products",
    )(outcomes, cohort, pre_end, post_start, unit_logit, time_logit)
    all_sums = lax.all_gather(sums, "unit", axis=0, tiled=True)
    width = unit_rows + day_cols
    pack, norms = pl.pallas_call(
        functools.partial(second_kernel, unit_devices),
        grid=(steps,),
        in_specs=[
            panel_spec,
            whole(unit_devices * 3 * groups, day_cols),
            end_spec,
            end_spec,
            whole(groups, unit_rows),
            days_spec,
        ],
        out_specs=[whole(2 * groups, width), whole(groups, lanes)],
        out_shape=[
            jax.ShapeDtypeStruct((2 * groups, width), f32),
            jax.ShapeDtypeStruct((groups, lanes), f32),
        ],
        compiler_params=params,
        name="unit_gradient",
    )(outcomes, all_sums, pre_end, post_start, cross, raised_days)
    all_pack = lax.all_gather(pack, "day", axis=0, tiled=True)
    updated, grads = pl.pallas_call(
        functools.partial(third_kernel, day_devices),
        grid=(steps,),
        in_specs=[
            panel_spec,
            whole(day_devices * 2 * groups, width),
            whole(groups, lanes),
            label_spec,
            group_spec,
            end_spec,
        ],
        out_specs=[group_spec, whole(2 * groups, day_cols)],
        out_shape=[
            jax.ShapeDtypeStruct((groups, unit_rows), f32),
            jax.ShapeDtypeStruct((2 * groups, day_cols), f32),
        ],
        compiler_params=params,
        name="time_gradient",
    )(outcomes, all_pack, norms, cohort, unit_logit, pre_end)
    all_grads = lax.all_gather(grads, ("unit", "day"), axis=0, tiled=True)
    return pl.pallas_call(
        functools.partial(fourth_kernel, unit_devices, day_devices),
        out_shape=[
            jax.ShapeDtypeStruct((groups, unit_rows), f32),
            jax.ShapeDtypeStruct((groups, day_cols), f32),
        ],
        compiler_params=params,
        name="new_weights",
    )(all_grads, updated, norms, all_pack, pre_end)


def solution(mesh):
    return jax.shard_map(
        local,
        mesh=mesh,
        in_specs=(P("unit", "day"), P("unit"), P(), P(), P(None, "unit"), P(None, "day")),
        out_specs=(P(None, "unit"), P(None, "day")),
        check_vma=False,
    )
```

time: 127 us -> 125 us (0.984)
  blocking collectives: 95.9 us -> 74.4 us
  waiting for transfers between devices: 0.01 us -> 18.2 us
  matrix products: 17.3 us -> 0 us
  between operations: 0.78 us -> 14.1 us
  Pallas kernels: 0 us -> 8.38 us
  starting transfers between devices: 5 us -> 0.04 us
  local copies, waits for them, and re-layouts: 6.11 us -> 9.41 us
  other arithmetic: 1.37 us -> 0 us
    psum x2 -> x0, blocking collectives: 79.3 us -> none  [the longest x1 40.5 us: local(): unit_total = lax.psum(jnp.sum(updated, axis=1), ('unit', 'day'))]
    all_gather x3 -> x2, blocking collectives: 16.6 us -> 74.4 us  [the longest x1 41.9 us: local(): all_grads = lax.all_gather(grads, ('unit', 'day'), axis=0, tiled=True)]
    all_gather x0 -> x1, waiting for transfers between devices: none -> 18.2 us  [local(): all_pack = lax.all_gather(pack, 'day', axis=0, tiled=True)]
    dot_general x6 -> x0, matrix products: 17.3 us -> none  [the longest x3 9.09 us: weigh_rows(): jnp.dot(left, outcomes, precision=highest, preferred_element_type=jnp.flo...]
    pallas_call x0 -> x4, Pallas kernels: none -> 8.38 us  [the longest x1 2.71 us: local(): pl.pallas_call(functools.partial(second_kernel, unit_devices), grid=(step...]
    unnamed x15 -> x16, local copies, waits for them, and re-layouts: 0.69 us -> 7.95 us
    all_to_all x1 -> x0, local copies, waits for them, and re-layouts: 5.43 us -> none  [local(): lax.all_to_all(outcomes, 'day', split_axis=0, concat_axis=1, tiled=True)]
    all_to_all x1 -> x0, starting transfers between devices: 5 us -> none  [local(): lax.all_to_all(outcomes, 'day', split_axis=0, concat_axis=1, tiled=True)]
  transfers between devices with their start and end apart: 1 -> 1, of which waited for: 0 -> 1; matrix products, arithmetic and copies ran while one was open for 5% -> 0% of each run, Pallas kernels for 0% -> 0%
where the time goes in v1:
time: 125 us; the launch traced here: 124 us
  blocking collectives  74.4 us (60%)
  waiting for transfers between devices  18.2 us (15%)
  between operations  14.1 us (11%)
  local copies, waits for them, and re-layouts  9.41 us (8%)
  Pallas kernels  8.38 us (7%)
    all_gather x1, blocking collectives, local(): all_grads = lax.all_gather(grads, ('unit', 'day'), axis=0, tiled=True)  41.9 us
    all_gather x1, blocking collectives, local(): all_sums = lax.all_gather(sums, 'unit', axis=0, tiled=True)  32.4 us
    all_gather x1, waiting for transfers between devices, local(): all_pack = lax.all_gather(pack, 'day', axis=0, tiled=True)  18.2 us
    unnamed x16, local copies, waits for them, and re-layouts  7.95 us
    pallas_call x1, Pallas kernels, local(): pl.pallas_call(functools.partial(second_kernel, unit_devices), grid=(step...  2.71 us
    pallas_call x1, Pallas kernels, local(): pl.pallas_call(functools.partial(first_kernel, day_devices * day_cols), g...  2.62 us
  transfers between devices with their start and end apart: 1, of which 1 were waited for; matrix products, arithmetic and copies ran while one was open for 0% of the time, Pallas kernels for 0%

profile of v1, /device:TPU:0, one launch (start us, length us, event | category | flops | bytes accessed | tf_op | source)
XLA Modules:
  0.0 124.4 jit_solution(15071943206878951991)
XLA Ops:
  7.2 0.0 all-gather.2.cloned.1.call-start
  7.2 0.7 copy.8.pre_end
  7.9 0.7 copy.9.post_start
  8.7 0.0 copy-start
  8.7 2.2 %copy-done = f32[4096,256]{1,0:T(8,128)S(1)} copy-done((f32[4096,256]{1,0:T(8,128)S(1)}, f32[4096,256]{1,0:T(8,128)}, u32[]{:S(2)}) %copy-start) | copy-done | bytes 4194328
  10.9 0.0 copy-start.3
  10.9 0.9 copy-done.3
  11.8 0.0 copy-start.5
  11.8 0.7 copy-done.5
  12.5 0.0 copy-start.7
  12.5 0.7 copy-done.7
  13.2 0.0 copy-start.4
  13.2 0.0 copy-start.6
  13.2 2.6 %first_products.1 = (f32[24,256]{1,0:T(8,128)S(1)}, f32[8,4096]{1,0:T(8,128)S(1)}, f32[8,256]{1,0:T(8,128)S(1)}) custom-call(f32[4096,256]{1,0:T(8,128)S(1)} %copy-done, s32[1,4096]{1,0:T(1,128)S(1)} %bitcast.3, s32[8,1]{1,0:T(8,128)S(1)} %copy.8.pre_end, s32[8,1]{1,0:T(8,128)S(1)} %copy.9.post_start, f32[8,4096]{1,0:T(8,128)S(1)} %copy-done.3, ...), custom_call_target="tpu_custom_call" | custom-call | tf_op jit(solution)/shard_map/first_products/pallas_call | solution.py:207
  15.8 32.4 %all_gather.9.sums = f32[192,256]{1,0:T(8,128)S(1)} all-gather(f32[24,256]{1,0:T(8,128)S(1)} %get-tuple-element.9), channel_id=1, replica_groups=mesh['unit'=8,'day'=4] {'unit'}, dimensions={0}, use_global_device_ids=true | all-gather | bytes 221184 | tf_op jit(solution)/shard_map/all_gather | solution.py:220
  48.2 2.7 %unit_gradient.1 = (f32[16,4352]{1,0:T(8,128)}, f32[8,128]{1,0:T(8,128)S(1)}) custom-call(f32[4096,256]{1,0:T(8,128)S(1)} %copy-done, f32[192,256]{1,0:T(8,128)S(1)} %all_gather.9.sums, s32[8,1]{1,0:T(8,128)S(1)} %copy.8.pre_end, s32[8,1]{1,0:T(8,128)S(1)} %copy.9.post_start, f32[8,4096]{1,0:T(8,128)S(1)} %get-tuple-element.10.cross, ...), custom_call_target="tpu_custom_call" | custom-call | tf_op jit(solution)/shard_map/unit_gradient/pallas_call | solution.py:222
  50.9 0.0 all-gather.2.cloned.1.call-update
  51.0 18.2 %all-gather.2.cloned.1.call-done.pack = f32[64,4352]{1,0:T(8,128)} async-done(((f32[16,4352]{1,0:T(8,128)}), f32[64,4352]{1,0:T(8,128)}) %all-gather.2.cloned.1.call-update) | async-done | bytes 1114128 | tf_op jit(solution)/shard_map/all_gather | solution.py:241
  69.2 0.0 copy-done.4
  69.2 0.0 copy-done.6
  69.2 0.0 copy-start.1
  69.2 2.2 %copy-done.1 = f32[4096,256]{1,0:T(8,128)S(1)} copy-done((f32[4096,256]{1,0:T(8,128)S(1)}, f32[4096,256]{1,0:T(8,128)}, u32[]{:S(2)}) %copy-start.1) | copy-done | bytes 4194328
  71.3 0.0 copy-start.2
  71.3 1.2 %copy-done.2 = f32[64,4352]{1,0:T(8,128)S(1)} copy-done((f32[64,4352]{1,0:T(8,128)S(1)}, f32[64,4352]{1,0:T(8,128)}, u32[]{:S(2)}) %copy-start.2) | copy-done | bytes 1114136
  72.6 2.1 %time_gradient.1 = (f32[8,4096]{1,0:T(8,128)S(1)}, f32[16,256]{1,0:T(8,128)S(1)}) custom-call(f32[4096,256]{1,0:T(8,128)S(1)} %copy-done.1, f32[64,4352]{1,0:T(8,128)S(1)} %copy-done.2, f32[8,128]{1,0:T(8,128)S(1)} %get-tuple-element.13.norms, s32[1,4096]{1,0:T(1,128)S(1)} %bitcast.4, f32[8,4096]{1,0:T(8,128)S(1)} %copy-done.4, s32[8,1]{1,0:T(8,128)S(1)} %copy.8.pre_end), custom_call_target="tpu_custom_call" | custom-call | tf_op jit(solution)/shard_map/time_gradient/pallas_call | solution.py:242
  74.7 41.9 %all_gather.11.gathered = f32[512,256]{1,0:T(8,128)S(1)} all-gather(f32[16,256]{1,0:T(8,128)S(1)} %get-tuple-element.14), channel_id=1, replica_groups=mesh['unit'=8,'day'=4] {'unit','day'}, dimensions={0}, use_global_device_ids=true | all-gather | bytes 540672 | tf_op jit(solution)/shard_map/all_gather | solution.py:261
  116.7 0.9 new_weights.1
Async XLA Ops:
  7.2 62.0 %all-gather.2.cloned.1.call-start = ((), (), s32[]{:S(2)}) async-start(), calls=%async_computation | async-start | bytes 1392640 | tf_op jit(solution)/shard_map/all_gather | solution.py:241
  8.7 2.2 %copy-start = (f32[4096,256]{1,0:T(8,128)S(1)}, f32[4096,256]{1,0:T(8,128)}, u32[]{:S(2)}) copy-start(f32[4096,256]{1,0:T(8,128)} %panel.5) | copy-start | bytes 12582916
  10.9 0.9 copy-start.3
  11.8 0.7 copy-start.5
  12.5 0.7 copy-start.7
  13.2 56.0 %copy-start.4 = (f32[8,4096]{1,0:T(8,128)S(1)}, f32[8,4096]{1,0:T(8,128)}, u32[]{:S(2)}) copy-start(f32[8,4096]{1,0:T(8,128)} %unit_logit.3) | copy-start | bytes 393220
  13.2 56.0 %copy-start.6 = (s32[4096]{0:T(1024)S(1)}, s32[4096]{0:T(1024)}, u32[]{:S(2)}) copy-start(s32[4096]{0:T(1024)} %param.7) | copy-start | bytes 49156
  69.2 2.2 %copy-start.1 = (f32[4096,256]{1,0:T(8,128)S(1)}, f32[4096,256]{1,0:T(8,128)}, u32[]{:S(2)}) copy-start(f32[4096,256]{1,0:T(8,128)} %panel.5) | copy-start | bytes 12582916
  71.3 1.2 %copy-start.2 = (f32[64,4352]{1,0:T(8,128)S(1)}, f32[64,4352]{1,0:T(8,128)}, u32[]{:S(2)}) copy-start(f32[64,4352]{1,0:T(8,128)} %all-gather.2.cloned.1.call-done.pack) | copy-start | bytes 3342340
Sparse Core Ops, SparseCore 0:
  51.1 18.0 all-gather.1
